TPU v7x, 32 devices: a whole 2x2x4 slice. The times are simulated.
32 devices in a mesh: grp: 4 (over y, core), feat: 8 (over z, x).
Axes of the slice: x: 2, y: 2, z: 4, core: 2. Of those that a mesh axis runs over, the one named last changes fastest.
Arguments:
- features: bfloat16 [128, 16384], P('feat', 'grp'), may hold values from -6 to 6
- w_self: bfloat16 [128, 256], replicated, may hold values from -0.5 to 0.5
- w_neigh: bfloat16 [128, 256], replicated, may hold values from -0.5 to 0.5
- bias: float32 [256], replicated, may hold values from -3 to 3
- tile_vals: bfloat16 [4, 8, 8, 128, 128], P('grp'), may hold values from -0.5 to 0.5
- tile_src: int32 [4, 8, 8], P('grp'), may hold values from 0 to 39, as said below
- tile_dst: int32 [4, 8, 8], P('grp'), may hold values from 0 to 3
- tile_count: int32 [4, 8], P('grp'), may hold values from 1 to 8, as said below
- hub_blocks: int32 [4, 2], P('grp'), may hold values from 0 to 31, as said below
- cotangent: bfloat16 [16384, 256], P(('grp', 'feat')), may hold values from -6 to 6
Outputs:
- output: bfloat16 [16384, 256], P(('grp', 'feat'))
- feat_grad: float32 [128, 16384], P('feat', 'grp')
- wself_grad: float32 [128, 256], P('feat')
- wneigh_grad: float32 [128, 256], P('feat')
- bias_grad: float32 [256], replicated
Inputs may be any that keep to these rules, and one draw needn't show every extreme that they name: `tile_src`: a slot number of the tile's own group's blocks below 32, or 32 plus a hub number. `tile_count`: some owner uses all 8 slots in every draw. `hub_blocks`: the 2 block numbers of a group are distinct.
All inputs are finite; a program needn't handle non-finite values.
Results may differ from a plain program's by a relative error of at most 0.0055.
Values may be sent and summed in bfloat16 or wider, within the bound.
A program may use at most 128 MiB of HBM per device.

v0:
```python
import jax
import jax.numpy as jnp
from jax import lax
from jax.sharding import PartitionSpec as P


def silu_parts(preact):
    sig = jax.nn.sigmoid(preact)
    return (preact * sig, sig * (1.0 + preact * (1.0 - sig)))


def contract_first(left, right):
    return lax.dot_general(
        left, right, (((0,), (0,)), ((), ())), preferred_element_type=jnp.float32
    )


def contract_last(left, right):
    return lax.dot_general(
        left, right, (((1,), (1,)), ((), ())), preferred_element_type=jnp.float32
    )


def local(
    features,
    w_self,
    w_neigh,
    bias,
    tile_vals,
    tile_src,
    tile_dst,
    tile_count,
    hub_blocks,
    cotangent,
):
    columns, group_nodes = features.shape
    owners = lax.axis_size("feat")
    position = lax.axis_index("feat")
    slot_count = tile_src.shape[2]
    tile_size = tile_vals.shape[-1]
    group_blocks = group_nodes // tile_size
    own_blocks = group_blocks // owners
    row_count = own_blocks * tile_size
    hub_ids = hub_blocks[0]
    highest = lax.Precision.HIGHEST
    own_hubs = jnp.take(
        features.reshape(columns, group_blocks, tile_size), hub_ids, axis=1
    ).reshape(columns, -1)
    all_hubs = lax.all_gather(own_hubs, "grp", axis=1, tiled=True)
    slot_total = group_blocks + all_hubs.shape[1] // tile_size
    upstream = cotangent.astype(jnp.float32)
    combined = jnp.concatenate([features, all_hubs], axis=1)
    full = lax.all_gather(combined, "feat", axis=0, tiled=True)
    feat_total = full.shape[0]
    values = lax.dynamic_index_in_dim(tile_vals[0], position, 0, keepdims=False)
    src_ids = lax.dynamic_index_in_dim(tile_src[0], position, 0, keepdims=False)
    dst_ids = lax.dynamic_index_in_dim(tile_dst[0], position, 0, keepdims=False)
    live_count = lax.dynamic_index_in_dim(tile_count[0], position, 0, keepdims=False)
    live_slots = (jnp.arange(slot_count, dtype=jnp.int32) < live_count).astype(jnp.float32)
    picked = jnp.take(full.reshape(feat_total, slot_total, tile_size), src_ids, axis=1)
    contrib = (
        jnp.einsum("tds,fts->ftd", values, picked, preferred_element_type=jnp.float32)
        * live_slots[None, :, None]
    )
    dst_hot = (dst_ids[:, None] == jnp.arange(own_blocks, dtype=jnp.int32)[None, :]).astype(
        jnp.float32
    )
    agg_own = (
        jnp.einsum("ftd,tb->fbd", contrib, dst_hot, precision=highest)
        .reshape(feat_total, row_count)
        .astype(jnp.bfloat16)
    )
    feat_own = lax.dynamic_slice_in_dim(full, position * row_count, row_count, 1)
    preact = contract_first(feat_own, w_self) + contract_first(agg_own, w_neigh) + bias
    activated, slope = silu_parts(preact)
    output = activated.astype(jnp.bfloat16)
    grad_pre = (upstream * slope).astype(jnp.bfloat16)
    wself_full = jnp.dot(feat_own, grad_pre, preferred_element_type=jnp.float32)
    wneigh_full = jnp.dot(agg_own, grad_pre, preferred_element_type=jnp.float32)
    bias_grad = jnp.sum(grad_pre.astype(jnp.float32), axis=0)
    wself_full, wneigh_full, bias_grad = lax.psum(
        (wself_full, wneigh_full, bias_grad), ("grp", "feat")
    )
    wself_grad = lax.dynamic_slice_in_dim(wself_full, position * columns, columns, 0)
    wneigh_grad = lax.dynamic_slice_in_dim(wneigh_full, position * columns, columns, 0)
    self_grad = contract_last(w_self, grad_pre)
    agg_grad = contract_last(w_neigh, grad_pre).astype(jnp.bfloat16)
    chosen = jnp.take(agg_grad.reshape(feat_total, own_blocks, tile_size), dst_ids, axis=1)
    src_grad = (
        jnp.einsum("tds,ftd->fts", values, chosen, preferred_element_type=jnp.float32)
        * live_slots[None, :, None]
    )
    src_hot = (src_ids[:, None] == jnp.arange(slot_total, dtype=jnp.int32)[None, :]).astype(
        jnp.float32
    )
    slot_grad = jnp.einsum("fts,tk->fks", src_grad, src_hot, precision=highest).reshape(
        feat_total, slot_total * tile_size
    )
    own_part = lax.dynamic_slice_in_dim(slot_grad, position * row_count, row_count, 1) + self_grad
    slot_grad = lax.dynamic_update_slice_in_dim(slot_grad, own_part, position * row_count, 1)
    mine = lax.psum_scatter(slot_grad, "feat", scatter_dimension=0, tiled=True)
    local_grad = mine[:, :group_nodes]
    hub_part = mine[:, group_nodes:]
    hub_back = (
        lax.psum_scatter(hub_part.astype(jnp.bfloat16), "grp", scatter_dimension=1, tiled=True)
        .astype(jnp.float32)
        .reshape(columns, -1, tile_size)
    )
    local_blocks = local_grad.reshape(columns, group_blocks, tile_size).at[:, hub_ids].add(hub_back)
    feat_grad = local_blocks.reshape(columns, group_nodes)
    return (output, feat_grad, wself_grad, wneigh_grad, bias_grad)


def solution(mesh):
    return jax.shard_map(
        local,
        mesh=mesh,
        in_specs=(
            P("feat", "grp"),
            P(),
            P(),
            P(),
            P("grp", None, None, None, None),
            P("grp", None, None),
            P("grp", None, None),
            P("grp", None),
            P("grp", None),
            P(("grp", "feat"), None),
        ),
        out_specs=(
            P(("grp", "feat"), None),
            P("feat", "grp"),
            P("feat", None),
            P("feat", None),
            P(),
        ),
        check_vma=False,
    )
```

profile of v0, /device:TPU:0, one launch (start us, length us, event | category | flops | bytes accessed | tf_op | source)
XLA Modules:
  0.0 304.6 jit_solution(11308443132222153842)
XLA Ops:
  7.2 0.0 all-gather.2.cloned.1.call-start
  7.2 0.8 fusion.38
  8.0 0.7 compare_and_fusion.2
  8.7 0.1 broadcast_bitcast_fusion
  8.8 0.9 copy_bitcast_fusion.3
  9.7 0.6 gather_fusion
  10.3 6.2 %all_gather.6 = bf16[16,1024]{1,0:T(8,128)(2,1)S(1)} all-gather(bf16[16,256]{1,0:T(8,128)(2,1)S(1)} %bitcast_select_fusion), channel_id=1, replica_groups=mesh['grp'=4,'feat'=8] {'grp'}, dimensions={1}, use_global_device_ids=true | all-gather | bytes 40960 | tf_op jit(solution)/shard_map/all_gather | solution.py:49
  16.5 1.6 pad_maximum_fusion
  18.1 0.0 all-reduce.3.cloned.1.call-start
  18.2 1.2 constant_dynamic-slice_fusion.3
  19.4 0.6 compare_convert_fusion
  20.1 0.7 fusion.39
  20.8 0.7 fusion.40
  21.5 0.7 compare_and_fusion
  22.2 39.8 %all-gather.2.cloned.1.call-done = bf16[128,5120]{1,0:T(8,128)(2,1)} async-done(((bf16[16,5120]{1,0:T(8,128)(2,1)}), bf16[128,5120]{1,0:T(8,128)(2,1)}) %all-gather.2.cloned.1.call-update) | async-done | bytes 1310736 | tf_op jit(solution)/shard_map/all_gather | solution.py:53
  62.0 1.8 copy.37
  63.8 1.4 copy.38
  65.2 2.0 gather_fusion.1
  67.2 0.4 fusion.1
  67.5 0.7 convolution_convert_fusion.1
  68.2 1.2 fusion.26
  69.4 1.2 convert_reduce_fusion
  70.6 0.9 fusion.17
  71.4 0.2 convolution_convert_fusion
  71.7 0.1 copy.40
  71.8 0.6 gather_fusion.2
  72.4 0.3 fusion
  72.7 1.3 fusion.4
  74.0 0.5 copy.73
  74.5 1.5 copy-done.1
  76.0 0.1 copy.47
  76.1 1.8 fusion.24
  77.9 0.0 reduce-scatter.3.cloned.1.call-start
  78.0 0.2 fusion.3
  78.2 0.1 copy.43
  78.3 0.8 constant_dynamic-update-slice_fusion
  79.1 0.0 reduce-scatter.5.cloned.1.call-start
  79.2 39.1 %psum.23 = f32[256]{0:T(256)} all-reduce(f32[256]{0:T(256)S(1)} %get-tuple-element.7), channel_id=1, replica_groups=mesh['grp'=4,'feat'=8] {'grp','feat'}, use_global_device_ids=true, to_apply=%region_6.7 | all-reduce | flops 256 | bytes 2048 | tf_op jit(solution)/shard_map/psum | solution.py:81
  118.2 83.7 %all-reduce.3.cloned.1.call-done = (f32[128,256]{1,0:T(8,128)}, f32[128,256]{1,0:T(8,128)}) async-done(((f32[128,256]{1,0:T(8,128)}, f32[128,256]{1,0:T(8,128)}), (f32[128,256]{1,0:T(8,128)}, f32[128,256]{1,0:T(8,128)})) %all-reduce.3.cloned.1.call-update) | async-done | bytes 262160 | tf_op jit(solution)/shard_map/psum | solution.py:81
  201.9 1.3 constant_dynamic-slice_fusion.1
  203.2 1.3 constant_dynamic-slice_fusion
  204.6 70.2 %reduce-scatter.3.cloned.1.call-done = f32[16,5120]{1,0:T(8,128)} async-done(((f32[128,5120]{1,0:T(8,128)}), f32[16,5120]{1,0:T(8,128)}) %reduce-scatter.3.cloned.1.call-update) | async-done | bytes 327696 | tf_op jit(solution)/shard_map/reduce_scatter | solution.py:101
  274.8 1.5 slice.19
  276.3 1.0 copy_bitcast_fusion.2
  277.3 18.7 %reduce-scatter.5.cloned.1.call-done = bf16[16,256]{1,0:T(8,128)(2,1)} async-done(((bf16[16,1024]{1,0:T(8,128)(2,1)}), bf16[16,256]{1,0:T(8,128)(2,1)}) %reduce-scatter.5.cloned.1.call-update) | async-done | bytes 8208 | tf_op jit(solution)/shard_map/reduce_scatter | solution.py:105
  296.0 0.7 reshape.194
  296.7 0.6 scatter_fusion
  297.3 0.7 copy_bitcast_fusion.1
  (21 shorter events, 0.1 us)
Async XLA Ops:
  7.2 60.0 %copy-start = (bf16[1,8,8,128,128]{4,3,2,1,0:T(8,128)(2,1)S(1)}, bf16[1,8,8,128,128]{4,3,2,1,0:T(8,128)(2,1)}, u32[]{:S(2)}) copy-start(bf16[1,8,8,128,128]{4,3,2,1,0:T(8,128)(2,1)} %param.14) | copy-start | bytes 6291460
  7.2 54.8 %all-gather.2.cloned.1.call-start = ((), (), s32[]{:S(2)}) async-start(), calls=%async_computation.2 | async-start | bytes 1474560 | tf_op jit(solution)/shard_map/all_gather | solution.py:53
  18.1 183.8 %all-reduce.3.cloned.1.call-start = ((), (), s32[]{:S(2)}) async-start(), calls=%async_computation.5 | async-start | bytes 524288 | tf_op jit(solution)/shard_map/psum | solution.py:81
  63.8 4.5 %copy-start.2 = (bf16[128,256]{1,0:T(8,128)(2,1)S(1)}, bf16[128,256]{1,0:T(8,128)(2,1)}, u32[]{:S(2)}) copy-start(bf16[128,256]{1,0:T(8,128)(2,1)} %param.11) | copy-start | bytes 196612
  65.2 4.2 %copy-start.3 = (bf16[128,256]{1,0:T(8,128)(2,1)S(1)}, bf16[128,256]{1,0:T(8,128)(2,1)}, u32[]{:S(2)}) copy-start(bf16[128,256]{1,0:T(8,128)(2,1)} %param.12) | copy-start | bytes 196612
  65.2 4.2 %copy-start.4 = (bf16[512,256]{1,0:T(8,128)(2,1)S(1)}, bf16[512,256]{1,0:T(8,128)(2,1)}, u32[]{:S(2)}) copy-start(bf16[512,256]{1,0:T(8,128)(2,1)} %param.19) | copy-start | bytes 786436
  65.2 4.2 %copy-start.5 = (f32[256]{0:T(256)S(1)}, f32[256]{0:T(256)}, u32[]{:S(2)}) copy-start(f32[256]{0:T(256)} %param.13) | copy-start | bytes 3076
  74.5 1.5 copy-start.1
  77.9 196.9 %reduce-scatter.3.cloned.1.call-start = ((), (), s32[]{:S(2)}) async-start(), calls=%async_computation.3 | async-start | bytes 2949120 | tf_op jit(solution)/shard_map/reduce_scatter | solution.py:101
  79.1 216.9 %reduce-scatter.5.cloned.1.call-start = ((), (), s32[]{:S(2)}) async-start(), calls=%async_computation.4 | async-start | bytes 40960 | tf_op jit(solution)/shard_map/reduce_scatter | solution.py:105
Sparse Core Ops, SparseCore 0:
  18.2 43.7 all-gather.1
  78.0 123.8 all-reduce.2
  205.4 69.3 reduce-scatter.2
  277.6 18.3 reduce-scatter.4
where the time goes:
time: 305 us
  waiting for transfers between devices  213 us (70%)
  blocking collectives  45.3 us (15%)
  local copies, waits for them, and re-layouts  18.2 us (6%)
  between operations  14 us (5%)
  matrix products  7.97 us (3%)
  other arithmetic  6.42 us (2%)
    psum x1, waiting for transfers between devices, local(): lax.psum((wself_full, wneigh_full, bias_grad), ('grp', 'feat'))  83.7 us
    reduce_scatter x1, waiting for transfers between devices, local(): mine = lax.psum_scatter(slot_grad, 'feat', scatter_dimension=0, tiled=True)  70.2 us
    all_gather x1, waiting for transfers between devices, local(): full = lax.all_gather(combined, 'feat', axis=0, tiled=True)  39.8 us
    psum x1, blocking collectives, local(): lax.psum((wself_full, wneigh_full, bias_grad), ('grp', 'feat'))  39.1 us
    reduce_scatter x1, waiting for transfers between devices, local(): lax.psum_scatter(hub_part.astype(jnp.bfloat16), 'grp', scatter_dimension=...  18.7 us
    all_gather x1, blocking collectives, local(): all_hubs = lax.all_gather(own_hubs, 'grp', axis=1, tiled=True)  6.23 us
  transfers between devices with their start and end apart: 4, of which 4 were waited for; matrix products, arithmetic and copies ran while one was open for 3% of the time, Pallas kernels for 0%

commit v1 on v0

--- a/solution.py
+++ b/solution.py
@@ -50,7 +50,16 @@
     slot_total = group_blocks + all_hubs.shape[1] // tile_size
     upstream = cotangent.astype(jnp.float32)
     combined = jnp.concatenate([features, all_hubs], axis=1)
-    full = lax.all_gather(combined, "feat", axis=0, tiled=True)
+    fan = lax.axis_size("feat")
+    tray = [(src_i, (src_i + 1) % fan) for src_i in range(fan)]
+    carry, e_now = ([combined], [combined])
+    in_order = [(src_i, (src_i - 1) % fan) for src_i in range(fan)]
+    for _ in range(fan // 2):
+        carry.append(lax.ppermute(carry[-1], "feat", tray))
+    for _ in [*range((fan - 1) // 2)]:
+        e_now.append(lax.ppermute(e_now[-1], "feat", in_order))
+    a_now = jnp.concatenate([*carry[::-1], *e_now[1:]], axis=0)
+    full = jnp.roll(a_now, (lax.axis_index("feat") - fan // 2) * combined.shape[0], axis=0)
     feat_total = full.shape[0]
     values = lax.dynamic_index_in_dim(tile_vals[0], position, 0, keepdims=False)
     src_ids = lax.dynamic_index_in_dim(tile_src[0], position, 0, keepdims=False)

time: 305 us -> 273 us (0.90)
  waiting for transfers between devices: 213 us -> 119 us
  local copies, waits for them, and re-layouts: 18.2 us -> 58.3 us
  starting transfers between devices: 0.16 us -> 16.4 us
  blocking collectives: 45.3 us -> 49.3 us
    reduce_scatter x1, waiting for transfers between devices: 70.2 us -> 0.01 us  [local(): mine = lax.psum_scatter(slot_grad, 'feat', scatter_dimension=0, tiled=True)]
    all_gather x1 -> x0, waiting for transfers between devices: 39.8 us -> none  [local(): full = lax.all_gather(combined, 'feat', axis=0, tiled=True)]
    concatenate x0 -> x3, local copies, waits for them, and re-layouts: none -> 21.7 us  [the longest x1 20.2 us: local(): jnp.roll(a_now, (lax.axis_index('feat') - fan // 2) * combined.shape[0],...]
    ppermute x0 -> x7, local copies, waits for them, and re-layouts: none -> 16.8 us  [the longest x4 9.61 us: local(): carry.append(lax.ppermute(carry[-1], 'feat', tray))]
    ppermute x0 -> x7, starting transfers between devices: none -> 16.3 us  [the longest x3 8.9 us: local(): e_now.append(lax.ppermute(e_now[-1], 'feat', in_order))]
    ppermute x0 -> x7, waiting for transfers between devices: none -> 9.39 us  [the longest x4 9.38 us: local(): carry.append(lax.ppermute(carry[-1], 'feat', tray))]
    psum x1, waiting for transfers between devices: 83.7 us -> 92.1 us  [local(): lax.psum((wself_full, wneigh_full, bias_grad), ('grp', 'feat'))]
    psum x1, blocking collectives: 39.1 us -> 43 us  [local(): lax.psum((wself_full, wneigh_full, bias_grad), ('grp', 'feat'))]
  transfers between devices with their start and end apart: 4 -> 10, of which waited for: 4 -> 5; matrix products, arithmetic and copies ran while one was open for 3% -> 9% of each run, Pallas kernels for 0% -> 0%
where the time goes in v1:
time: 273 us; the launch traced here: 271 us
  waiting for transfers between devices  119 us (44%)
  local copies, waits for them, and re-layouts  58.3 us (21%)
  blocking collectives  49.3 us (18%)
  starting transfers between devices  16.4 us (6%)
  between operations  15.8 us (6%)
  matrix products  8.21 us (3%)
  other arithmetic  4.02 us (1%)
    psum x1, waiting for transfers between devices, local(): lax.psum((wself_full, wneigh_full, bias_grad), ('grp', 'feat'))  92.1 us
    psum x1, blocking collectives, local(): lax.psum((wself_full, wneigh_full, bias_grad), ('grp', 'feat'))  43 us
    concatenate x1, local copies, waits for them, and re-layouts, local(): jnp.roll(a_now, (lax.axis_index('feat') - fan // 2) * combined.shape[0],...  20.2 us
    reduce_scatter x1, waiting for transfers between devices, local(): lax.psum_scatter(hub_part.astype(jnp.bfloat16), 'grp', scatter_dimension=...  17.5 us
    ppermute x4, local copies, waits for them, and re-layouts, local(): carry.append(lax.ppermute(carry[-1], 'feat', tray))  9.61 us
    ppermute x4, waiting for transfers between devices, local(): carry.append(lax.ppermute(carry[-1], 'feat', tray))  9.38 us
    ppermute x3, starting transfers between devices, local(): e_now.append(lax.ppermute(e_now[-1], 'feat', in_order))  8.9 us
    ppermute x4, starting transfers between devices, local(): carry.append(lax.ppermute(carry[-1], 'feat', tray))  7.39 us
  transfers between devices with their start and end apart: 10, of which 5 were waited for; matrix products, arithmetic and copies ran while one was open for 9% of the time, Pallas kernels for 0%

profile of v1, /device:TPU:0, one launch (start us, length us, event | category | flops | bytes accessed | tf_op | source)
XLA Modules:
  0.0 271.0 jit_solution(16599675943716961695)
XLA Ops:
  8.1 1.1 constant_dynamic-update-slice_fusion.1
  9.1 0.9 copy_bitcast_fusion.3
  10.0 0.7 compare_and_fusion.2
  10.7 0.7 fusion.36
  12.0 6.2 %all_gather.3 = bf16[16,1024]{1,0:T(8,128)(2,1)S(1)} all-gather(bf16[16,256]{1,0:T(8,128)(2,1)S(1)} %bitcast_select_fusion), channel_id=1, replica_groups=mesh['grp'=4,'feat'=8] {'grp'}, dimensions={1}, use_global_device_ids=true | all-gather | bytes 40960 | tf_op jit(solution)/shard_map/all_gather | solution.py:49
  18.3 1.9 collective-permute-start
  20.2 3.1 %collective-permute-start.4 = (bf16[16,5120]{1,0:T(8,128)(2,1)S(1)}, bf16[16,5120]{1,0:T(8,128)(2,1)S(1)}, u32[]{:S(2)}, u32[]{:S(2)}) collective-permute-start(bf16[16,5120]{1,0:T(8,128)(2,1)S(1)} %constant_dynamic-update-slice_fusion), channel_id=1, source_target_pairs={{0,7},{1,0},{2,1},{3,2},{4,3},{5,4},{6,5},{7,6},{8,15},{9,8},{10,9... | collective-permute-start | bytes 491528 | tf_op jit(solution)/shard_map/ppermute | solution.py:60
  23.3 4.8 %collective-permute-done = bf16[16,5120]{1,0:T(8,128)(2,1)S(1)} collective-permute-done((bf16[16,5120]{1,0:T(8,128)(2,1)S(1)}, bf16[16,5120]{1,0:T(8,128)(2,1)S(1)}, u32[]{:S(2)}, u32[]{:S(2)}) %collective-permute-start) | collective-permute-done | bytes 163872 | tf_op jit(solution)/shard_map/ppermute | solution.py:58
  28.0 2.1 collective-permute-start.1
  30.1 0.7 compare_and_fusion
  30.9 3.1 %collective-permute-start.5 = (bf16[16,5120]{1,0:T(8,128)(2,1)S(1)}, bf16[16,5120]{1,0:T(8,128)(2,1)}, u32[]{:S(2)}, u32[]{:S(2)}) collective-permute-start(bf16[16,5120]{1,0:T(8,128)(2,1)S(1)} %collective-permute-done.4), channel_id=1, source_target_pairs={{0,7},{1,0},{2,1},{3,2},{4,3},{5,4},{6,5},{7,6},{8,15},{9,8},{10,9... | collective-permute-start | bytes 491528 | tf_op jit(solution)/shard_map/ppermute | solution.py:60
  34.0 3.2 %collective-permute-done.1 = bf16[16,5120]{1,0:T(8,128)(2,1)S(1)} collective-permute-done((bf16[16,5120]{1,0:T(8,128)(2,1)S(1)}, bf16[16,5120]{1,0:T(8,128)(2,1)S(1)}, u32[]{:S(2)}, u32[]{:S(2)}) %collective-permute-start.1) | collective-permute-done | bytes 163872 | tf_op jit(solution)/shard_map/ppermute | solution.py:58
  37.2 2.1 collective-permute-start.2
  39.3 0.7 fusion.37
  40.0 1.2 constant_dynamic-slice_fusion.3
  41.3 2.7 collective-permute-start.6
  43.9 1.4 collective-permute-done.2
  45.4 1.3 collective-permute-start.3
  46.6 0.7 compare_convert_fusion
  47.3 1.5 copy.41
  48.8 2.4 copy.40
  51.2 2.4 copy.42
  53.6 2.4 copy.39
  56.0 2.5 copy.43
  58.5 2.4 copy.38
  60.9 2.4 copy.44
  63.3 2.4 copy.37
  65.7 20.2 %concatenate.10 = bf16[256,5120]{0,1:T(8,128)(2,1)} concatenate(bf16[16,5120]{0,1:T(8,128)(2,1)} %copy.37, bf16[16,5120]{0,1:T(8,128)(2,1)} %copy.38, bf16[16,5120]{0,1:T(8,128)(2,1)} %copy.39, bf16[16,5120]{0,1:T(8,128)(2,1)} %copy.40, bf16[16,5120]{0,1:T(8,128)(2,1)S(1)} %copy.41, bf16[16,5120]{0,1:T(8,128)(2,1)} %copy.42, bf16[16,5120]{0,1:T(8,128)(2,1)} %copy.43, ...), dimensions={0} | concatenate | bytes 5242880 | tf_op jit(solution)/shard_map/jit(_roll_dynamic)/concatenate | solution.py:62
  85.9 2.2 constant_dynamic-slice_fusion.4
  88.1 1.5 copy.53
  89.6 2.0 gather_fusion.1
  91.9 0.7 convolution_convert_fusion.1
  92.9 2.1 convert_reduce_fusion
  95.2 1.9 fusion.25
  97.2 0.8 fusion.17
  99.0 1.3 fusion.4
  100.8 1.5 copy-done.1
  102.9 0.8 constant_dynamic-update-slice_fusion.2
  103.8 43.0 %psum.23 = f32[256]{0:T(256)} all-reduce(f32[256]{0:T(256)S(1)} %get-tuple-element.7), channel_id=1, replica_groups=mesh['grp'=4,'feat'=8] {'grp','feat'}, use_global_device_ids=true, to_apply=%region_6.7 | all-reduce | flops 256 | bytes 2048 | tf_op jit(solution)/shard_map/psum | solution.py:90
  146.8 92.1 %all-reduce.3.cloned.1.call-done = (f32[128,256]{1,0:T(8,128)}, f32[128,256]{1,0:T(8,128)}) async-done(((f32[128,256]{1,0:T(8,128)}, f32[128,256]{1,0:T(8,128)}), (f32[128,256]{1,0:T(8,128)}, f32[128,256]{1,0:T(8,128)})) %all-reduce.3.cloned.1.call-update) | async-done | bytes 262160 | tf_op jit(solution)/shard_map/psum | solution.py:90
  238.9 1.3 constant_dynamic-slice_fusion.1
  240.2 1.3 constant_dynamic-slice_fusion
  241.6 1.5 slice.19
  243.1 1.0 copy_bitcast_fusion.2
  244.0 17.5 %reduce-scatter.5.cloned.1.call-done = bf16[16,256]{1,0:T(8,128)(2,1)} async-done(((bf16[16,1024]{1,0:T(8,128)(2,1)}), bf16[16,256]{1,0:T(8,128)(2,1)}) %reduce-scatter.5.cloned.1.call-update) | async-done | bytes 8208 | tf_op jit(solution)/shard_map/reduce_scatter | solution.py:114
  261.5 0.7 reshape.194
  262.2 0.6 scatter_fusion
  262.9 0.7 copy_bitcast_fusion.1
  (49 shorter events, 3.7 us)
Async XLA Ops:
  8.0 83.5 %copy-start = (bf16[1,8,8,128,128]{4,3,2,1,0:T(8,128)(2,1)S(1)}, bf16[1,8,8,128,128]{4,3,2,1,0:T(8,128)(2,1)}, u32[]{:S(2)}) copy-start(bf16[1,8,8,128,128]{4,3,2,1,0:T(8,128)(2,1)} %param.14) | copy-start | bytes 6291460
  8.0 230.9 %all-reduce.3.cloned.1.call-start = ((), (), s32[]{:S(2)}) async-start(), calls=%async_computation.4 | async-start | bytes 524288 | tf_op jit(solution)/shard_map/psum | solution.py:90
  18.3 28.4 %copy-start.2 = (bf16[16,5120]{1,0:T(8,128)(2,1)}, bf16[16,5120]{1,0:T(8,128)(2,1)S(1)}, u32[]{:S(2)}) copy-start(bf16[16,5120]{1,0:T(8,128)(2,1)S(1)} %constant_dynamic-update-slice_fusion) | copy-start | bytes 491524
  18.3 9.8 %collective-permute-start = (bf16[16,5120]{1,0:T(8,128)(2,1)S(1)}, bf16[16,5120]{1,0:T(8,128)(2,1)S(1)}, u32[]{:S(2)}, u32[]{:S(2)}) collective-permute-start(bf16[16,5120]{1,0:T(8,128)(2,1)S(1)} %constant_dynamic-update-slice_fusion), channel_id=1, source_target_pairs={{0,1},{1,2},{2,3},{3,4},{4,5},{5,6},{6,7},{7,0},{8,9},{9,10},{10,1... | collective-permute-start | bytes 491528 | tf_op jit(solution)/shard_map/ppermute | solution.py:58
  20.2 10.7 %collective-permute-start.4 = (bf16[16,5120]{1,0:T(8,128)(2,1)S(1)}, bf16[16,5120]{1,0:T(8,128)(2,1)S(1)}, u32[]{:S(2)}, u32[]{:S(2)}) collective-permute-start(bf16[16,5120]{1,0:T(8,128)(2,1)S(1)} %constant_dynamic-update-slice_fusion), channel_id=1, source_target_pairs={{0,7},{1,0},{2,1},{3,2},{4,3},{5,4},{6,5},{7,6},{8,15},{9,8},{10,9... | collective-permute-start | bytes 491528 | tf_op jit(solution)/shard_map/ppermute | solution.py:60
  28.0 18.6 %copy-start.4 = (bf16[16,5120]{1,0:T(8,128)(2,1)}, bf16[16,5120]{1,0:T(8,128)(2,1)S(1)}, u32[]{:S(2)}) copy-start(bf16[16,5120]{1,0:T(8,128)(2,1)S(1)} %collective-permute-done) | copy-start | bytes 491524
  28.0 9.2 %collective-permute-start.1 = (bf16[16,5120]{1,0:T(8,128)(2,1)S(1)}, bf16[16,5120]{1,0:T(8,128)(2,1)S(1)}, u32[]{:S(2)}, u32[]{:S(2)}) collective-permute-start(bf16[16,5120]{1,0:T(8,128)(2,1)S(1)} %collective-permute-done), channel_id=1, source_target_pairs={{0,1},{1,2},{2,3},{3,4},{4,5},{5,6},{6,7},{7,0},{8,9},{9,10},{10,1... | collective-permute-start | bytes 491528 | tf_op jit(solution)/shard_map/ppermute | solution.py:58
  30.9 15.8 %copy-start.5 = (bf16[16,5120]{1,0:T(8,128)(2,1)}, bf16[16,5120]{1,0:T(8,128)(2,1)S(1)}, u32[]{:S(2)}) copy-start(bf16[16,5120]{1,0:T(8,128)(2,1)S(1)} %collective-permute-done.4) | copy-start | bytes 491524
  30.9 10.4 %collective-permute-start.5 = (bf16[16,5120]{1,0:T(8,128)(2,1)S(1)}, bf16[16,5120]{1,0:T(8,128)(2,1)}, u32[]{:S(2)}, u32[]{:S(2)}) collective-permute-start(bf16[16,5120]{1,0:T(8,128)(2,1)S(1)} %collective-permute-done.4), channel_id=1, source_target_pairs={{0,7},{1,0},{2,1},{3,2},{4,3},{5,4},{6,5},{7,6},{8,15},{9,8},{10,9... | collective-permute-start | bytes 491528 | tf_op jit(solution)/shard_map/ppermute | solution.py:60
  37.2 9.4 %copy-start.6 = (bf16[16,5120]{1,0:T(8,128)(2,1)}, bf16[16,5120]{1,0:T(8,128)(2,1)S(1)}, u32[]{:S(2)}) copy-start(bf16[16,5120]{1,0:T(8,128)(2,1)S(1)} %collective-permute-done.1) | copy-start | bytes 491524
  37.2 8.2 %collective-permute-start.2 = (bf16[16,5120]{1,0:T(8,128)(2,1)S(1)}, bf16[16,5120]{1,0:T(8,128)(2,1)}, u32[]{:S(2)}, u32[]{:S(2)}) collective-permute-start(bf16[16,5120]{1,0:T(8,128)(2,1)S(1)} %collective-permute-done.1), channel_id=1, source_target_pairs={{0,1},{1,2},{2,3},{3,4},{4,5},{5,6},{6,7},{7,0},{8,9},{9,10},{10,1... | collective-permute-start | bytes 491528 | tf_op jit(solution)/shard_map/ppermute | solution.py:58
  41.3 19.7 %collective-permute-start.6 = (bf16[16,5120]{1,0:T(8,128)(2,1)}, bf16[16,5120]{1,0:T(8,128)(2,1)}, u32[]{:S(2)}, u32[]{:S(2)}) collective-permute-start(bf16[16,5120]{1,0:T(8,128)(2,1)} %collective-permute-done.5), channel_id=1, source_target_pairs={{0,7},{1,0},{2,1},{3,2},{4,3},{5,4},{6,5},{7,6},{8,15},{9,8},{10,9... | collective-permute-start | bytes 491528 | tf_op jit(solution)/shard_map/ppermute | solution.py:60
  45.4 17.9 %collective-permute-start.3 = (bf16[16,5120]{1,0:T(8,128)(2,1)}, bf16[16,5120]{1,0:T(8,128)(2,1)}, u32[]{:S(2)}, u32[]{:S(2)}) collective-permute-start(bf16[16,5120]{1,0:T(8,128)(2,1)} %collective-permute-done.2), channel_id=1, source_target_pairs={{0,1},{1,2},{2,3},{3,4},{4,5},{5,6},{6,7},{7,0},{8,9},{9,10},{10,1... | collective-permute-start | bytes 491528 | tf_op jit(solution)/shard_map/ppermute | solution.py:58
  88.1 4.5 %copy-start.3 = (bf16[128,256]{1,0:T(8,128)(2,1)S(1)}, bf16[128,256]{1,0:T(8,128)(2,1)}, u32[]{:S(2)}) copy-start(bf16[128,256]{1,0:T(8,128)(2,1)} %param.12) | copy-start | bytes 196612
  89.6 3.3 %copy-start.7 = (bf16[128,256]{1,0:T(8,128)(2,1)S(1)}, bf16[128,256]{1,0:T(8,128)(2,1)}, u32[]{:S(2)}) copy-start(bf16[128,256]{1,0:T(8,128)(2,1)} %param.11) | copy-start | bytes 196612
  89.6 3.3 %copy-start.8 = (bf16[512,256]{1,0:T(8,128)(2,1)S(1)}, bf16[512,256]{1,0:T(8,128)(2,1)}, u32[]{:S(2)}) copy-start(bf16[512,256]{1,0:T(8,128)(2,1)} %param.19) | copy-start | bytes 786436
  89.6 3.3 %copy-start.9 = (f32[256]{0:T(256)S(1)}, f32[256]{0:T(256)}, u32[]{:S(2)}) copy-start(f32[256]{0:T(256)} %param.13) | copy-start | bytes 3076
  100.8 1.5 copy-start.1
  102.5 139.1 %reduce-scatter.3.cloned.1.call-start = ((), (), s32[]{:S(2)}) async-start(), calls=%async_computation.2 | async-start | bytes 2949120 | tf_op jit(solution)/shard_map/reduce_scatter | solution.py:110
  103.7 157.8 %reduce-scatter.5.cloned.1.call-start = ((), (), s32[]{:S(2)}) async-start(), calls=%async_computation.3 | async-start | bytes 40960 | tf_op jit(solution)/shard_map/reduce_scatter | solution.py:114
Sparse Core Ops, SparseCore 0:
  102.6 136.2 all-reduce.2
Sparse Core Ops, SparseCore 1:
  106.5 72.4 reduce-scatter.2
  243.1 18.3 reduce-scatter.4
